TPU v7x, 32 devices: a whole 2x2x4 slice. The times are simulated.
32 devices in a mesh: facet: 8 (over y, x, core), col: 4 (over z).
Axes of the slice: x: 2, y: 2, z: 4, core: 2. Of those that a mesh axis runs over, the one named last changes fastest.
Arguments:
- strips: float32 [8, 2, 192, 2048], P('facet', None, 'col'), may hold values from -6 to 6
- sub_offset: int32 [4, 8], replicated, may hold values from 0 to 2047
- uv_cells: int32 [4, 8, 2, 128], P('col', 'facet'), may hold values from 0 to 255
- measured: float32 [4, 8, 2, 128], P('col', 'facet'), may hold values from -6 to 6
Outputs:
- dirty_image: float32 [8, 2, 192, 2048], P('facet', None, 'col')
- residual_vis: float32 [4, 8, 2, 128], P('col', 'facet')
All inputs are finite; a program needn't handle non-finite values.
Results may differ from a plain program's by a relative error of at most 0.0003.
Values sent between devices are 32-bit elements; how exact they have to be, the bound alone decides.
A program may use at most 64 MiB of HBM per device.

v0:
```python
import math

import jax
import jax.numpy as jnp
import numpy as np
from jax import lax
from jax.sharding import PartitionSpec as P

SUBGRID_SIZE = 256
HIGH = lax.Precision.HIGH


def unit(numer, denom):
    angle = (np.asarray(numer) % denom) * (2.0 * math.pi / denom)
    return np.exp(1j * angle)


def pick_table(facets, width):
    total = facets * width
    cells = np.arange(SUBGRID_SIZE)
    factor = (facets * width * width) ** -0.25
    e = factor * unit(np.arange(total)[:, None] * cells[None, :], total)
    h = e @ unit(-cells[:, None] * cells[None, :], SUBGRID_SIZE)
    h = h.reshape(facets, width, SUBGRID_SIZE)
    return np.concatenate([h.real, h.imag], axis=1).astype(np.float32)


def dot(a, b):
    return jnp.dot(a, b, precision=HIGH, preferred_element_type=jnp.float32)


def body(strips, sub_offset, uv_cells, measured):
    facets = lax.axis_size("facet")
    ncol = lax.axis_size("col")
    f = lax.axis_index("facet")
    c = lax.axis_index("col")
    width, length = strips.shape[2], strips.shape[3]
    per_col = sub_offset.shape[1]
    vis = uv_cells.shape[3]
    rows_all = width * ncol
    xr, xi = strips[0, 0], strips[0, 1]

    uv = lax.all_gather(uv_cells, "facet", axis=1, tiled=True)
    uv = lax.all_gather(uv, "col", axis=0, tiled=True)
    h = lax.dynamic_index_in_dim(jnp.asarray(pick_table(facets, width)), f, 0, keepdims=False)
    cells = jnp.arange(SUBGRID_SIZE, dtype=jnp.int32)[:, None]
    pick_u = (cells == uv[:, :, 0].reshape(1, -1)).astype(jnp.float32)
    pick_v = (cells == uv[:, :, 1].reshape(1, -1)).astype(jnp.float32)
    gv = dot(h, pick_v).reshape(2, width, ncol, per_col, vis)
    own_u = lax.dynamic_slice_in_dim(pick_u, c * per_col * vis, per_col * vis, 1)
    gu = dot(h, own_u).reshape(2, width, per_col, vis)
    own_v = lax.dynamic_index_in_dim(gv, c, 2, keepdims=False)

    j = jnp.arange(length, dtype=jnp.int32)
    ang = ((sub_offset.reshape(-1, 1) * j[None, :]) % length).astype(jnp.float32) * (2.0 * math.pi / length)
    pr, pi = jnp.cos(ang), jnp.sin(ang)
    w = unit(np.arange(length)[:, None] * np.arange(width)[None, :], length) / math.sqrt(length)
    wr, wi = np.real(w).astype(np.float32), np.imag(w).astype(np.float32)
    opr = lax.dynamic_slice_in_dim(pr, c * per_col, per_col, 0)[:, None, :]
    opi = lax.dynamic_slice_in_dim(pi, c * per_col, per_col, 0)[:, None, :]
    sr = (xr[None] * opr + xi[None] * opi).reshape(per_col * width, length)
    si = (xi[None] * opr - xr[None] * opi).reshape(per_col * width, length)
    wide = np.concatenate([wr, -wi], axis=1), np.concatenate([wi, wr], axis=1)
    k = dot(sr, wide[0]) + dot(si, wide[1])
    kr = k[:, :width].reshape(per_col, width, width)
    ki = k[:, width:].reshape(per_col, width, width)

    def bdot(a, b):
        return jnp.einsum("skl,lsv->skv", a, b, precision=HIGH, preferred_element_type=jnp.float32)

    ar = bdot(kr, own_v[0]) - bdot(ki, own_v[1])
    ai = bdot(kr, own_v[1]) + bdot(ki, own_v[0])
    gur, gui = gu[0].transpose(1, 0, 2), gu[1].transpose(1, 0, 2)
    part_r = jnp.sum(ar * gur - ai * gui, axis=1) / SUBGRID_SIZE
    part_i = jnp.sum(ar * gui + ai * gur, axis=1) / SUBGRID_SIZE
    part = -jnp.stack([part_r, part_i], axis=1)
    per_dev = measured.shape[1]
    mine = lax.dynamic_slice_in_dim(part, f * per_dev, per_dev, 0) + measured[0]
    part = lax.dynamic_update_slice_in_dim(part, mine, f * per_dev, 0)
    every = jnp.zeros((ncol,) + part.shape, jnp.float32)
    every = lax.dynamic_update_slice_in_dim(every, part[None], c, 0)
    res = lax.psum(every, ("facet", "col"))
    residual_vis = lax.dynamic_slice(res, (c, f * per_dev, 0, 0), (1, per_dev, 2, vis))

    r = np.arange(rows_all)
    p = unit(r[:, None] * r[None, :], rows_all) / math.sqrt(rows_all)
    p = p.reshape(ncol, width, ncol, width).transpose(0, 2, 1, 3)
    pmr = np.concatenate([p.real, p.imag], axis=3)
    pmi = np.concatenate([p.imag, -p.real], axis=3)
    pm = np.concatenate([pmr, pmi], axis=2).astype(np.float32)
    pm = lax.dynamic_index_in_dim(jnp.asarray(pm), c, 0, keepdims=False)
    ph = dot(pm.reshape(ncol * 2 * width, 2 * width), h).reshape(ncol, 2 * width, SUBGRID_SIZE)
    pg = jnp.einsum(
        "cru,ucx->crx", ph, pick_u.reshape(SUBGRID_SIZE, ncol, per_col * vis),
        precision=HIGH, preferred_element_type=jnp.float32,
    ).reshape(ncol, 2, width, per_col, vis)
    rr, ri = res[:, None, :, 0], res[:, None, :, 1]
    qr = pg[:, 0] * rr - pg[:, 1] * ri
    qi = pg[:, 0] * ri + pg[:, 1] * rr
    q = jnp.concatenate([qr, qi], axis=1)

    def adot(a, b):
        return jnp.einsum("crsv,lcsv->cslr", a, b, precision=HIGH, preferred_element_type=jnp.float32)

    dgr, dgi = adot(q, gv[0]), adot(q, gv[1])
    dr = dgr[..., :width] + dgi[..., width:]
    di = dgr[..., width:] - dgi[..., :width]
    left = jnp.concatenate([dr, di], -1).reshape(ncol, -1, 2 * width)
    right = jnp.concatenate([-di, dr], -1).reshape(ncol, -1, 2 * width)

    def add_column(acc, item):
        l, r, cr, ci = item
        vr = (cr[:, None, :] * wr.T[None] - ci[:, None, :] * wi.T[None]).reshape(-1, length)
        vi = (cr[:, None, :] * wi.T[None] + ci[:, None, :] * wr.T[None]).reshape(-1, length)
        return acc + dot(l.T, vr) + dot(r.T, vi), None

    shape = (ncol, per_col, length)
    image, _ = lax.scan(
        add_column,
        jnp.zeros((2 * width, length), jnp.float32),
        (left, right, pr.reshape(shape), pi.reshape(shape)),
    )
    return image.reshape(1, 2, width, length), residual_vis


def solution(mesh):
    return jax.shard_map(
        body,
        mesh=mesh,
        in_specs=(
            P("facet", None, "col", None),
            P(),
            P("col", "facet", None, None),
            P("col", "facet", None, None),
        ),
        out_specs=(P("facet", None, "col", None), P("col", "facet", None, None)),
        check_vma=False,
    )
```

profile of v0, /device:TPU:0, one launch (start us, length us, event | category | flops | bytes accessed | tf_op | source)
XLA Modules:
  0.0 136.9 jit_solution(10468650770285900959)
XLA Ops:
  4.3 1.5 %fusion.55 = f32[384,96]{0,1:T(8,128)S(1)} fusion(f32[384,2048]{1,0:T(8,128)S(1)} %bitcast.180, f32[2048,96]{1,0:T(8,128)S(1)} %copy-done.2), kind=kOutput, calls=%fused_computation.113 | convolution fusion | flops 452984832 | bytes 4079616 | tf_op jit(solution)/shard_map/dot_general | solution.py:29
  5.8 1.6 %convolution_add_fusion.3 = f32[384,96]{0,1:T(8,128)S(1)} fusion(f32[384,96]{0,1:T(8,128)S(1)} %fusion.55, f32[384,2048]{1,0:T(8,128)S(1)} %bitcast.179, f32[2048,96]{1,0:T(8,128)S(1)} %copy-done.1), kind=kOutput, calls=%fused_computation.25 | convolution fusion | flops 453021696 | bytes 4227072 | tf_op jit(solution)/shard_map/dot_general | solution.py:29
  8.2 10.4 %all_gather.6 = s32[1,8,2,128]{3,2,0,1:T(2,128)S(1)} all-gather(s32[1,1,2,128]{3,2,0,1:T(2,128)S(1)} %bitcast.197), channel_id=1, replica_groups=mesh['facet'=8,'col'=4] {'facet'}, dimensions={1}, use_global_device_ids=true | all-gather | bytes 9216 | tf_op jit(solution)/shard_map/all_gather | solution.py:43
  18.6 13.3 %all_gather.7 = s32[4,8,2,128]{3,1,2,0:T(8,128)S(1)} all-gather(s32[1,8,2,128]{3,1,2,0:T(8,128)S(1)} %copy.39), channel_id=1, replica_groups=mesh['facet'=8,'col'=4] {'col'}, dimensions={0}, use_global_device_ids=true | all-gather | bytes 40960 | tf_op jit(solution)/shard_map/all_gather | solution.py:44
  32.5 2.2 %fusion.6 = f32[96,4096]{1,0:T(8,128)S(1)} fusion(s32[4096]{0:T(1024)S(1)} %get-tuple-element.169, f32[8,96,256]{2,1,0:T(8,128)} %constant.84.clone, s32[]{:T(128)S(6)} %select_n.33), kind=kOutput, calls=%fused_computation.14 | convolution fusion | flops 605028352 | bytes 1687556 | tf_op jit(solution)/shard_map/dot_general | solution.py:29
  42.4 39.7 %psum.7 = f32[4,8,2,128]{3,2,1,0:T(2,128)S(1)} all-reduce(f32[4,8,2,128]{3,2,1,0:T(2,128)S(1)} %constant_dynamic-update-slice_fusion), channel_id=1, replica_groups=mesh['facet'=8,'col'=4] {'facet','col'}, use_global_device_ids=true, to_apply=%region_2.3 | all-reduce | flops 8192 | bytes 65536 | tf_op jit(solution)/shard_map/psum | solution.py:82
  82.1 1.3 fusion.36
  85.8 1.6 %fusion.11 = f32[4,8,48,96]{3,2,1,0:T(8,128)S(1)} fusion(f32[4,48,8,128]{3,1,2,0:T(8,128)S(1)} %get-tuple-element.145, f32[4,48,8,128]{3,1,2,0:T(8,128)S(1)} %get-tuple-element.144, f32[48,4,8,128]{3,2,1,0:T(8,128)S(1)} %bitcast.186), kind=kOutput, calls=%fused_computation.22 | convolution fusion | flops 113639424 | bytes 2949120 | tf_op jit(solution)/shard_map/crsv,lcsv->cslr/dot_general | solution.py:103
  87.5 1.6 %fusion.10 = f32[4,8,48,96]{3,2,1,0:T(8,128)S(1)} fusion(f32[4,48,8,128]{3,1,2,0:T(8,128)S(1)} %get-tuple-element.145, f32[4,48,8,128]{3,1,2,0:T(8,128)S(1)} %get-tuple-element.144, f32[48,4,8,128]{3,2,1,0:T(8,128)S(1)} %bitcast.185), kind=kOutput, calls=%fused_computation.21 | convolution fusion | flops 113639424 | bytes 2949120 | tf_op jit(solution)/shard_map/crsv,lcsv->cslr/dot_general | solution.py:103
  89.6 1.6 %pad_maximum_fusion.4 = (f32[4,8,48,96]{3,2,1,0:T(8,128)}, f32[4,8,48,96]{3,2,1,0:T(8,128)}) fusion(f32[4,8,48,48]{3,2,1,0:T(8,128)S(1)} %get-tuple-element.146, f32[4,8,48,48]{3,2,1,0:T(8,128)S(1)} %get-tuple-element.138, f32[4,8,48,48]{3,2,1,0:T(8,128)S(1)} %get-tuple-element.139), kind=kLoop, calls=%fused_computation.33 | loop fusion | flops 294912 | bytes 2064384 | tf_op jit(solution)/shard_map/concatenate | solution.py:109
  91.2 1.9 %fusion.41 = (f32[4,8,2048]{2,1,0:T(8,128)}, f32[4,8,2048]{2,1,0:T(8,128)}) fusion(s32[4,8]{1,0:T(4,128)S(1)} %copy-done.4), kind=kLoop, calls=%fused_computation.82 | loop fusion | flops 917504 | bytes 524416 | tf_op jit(solution)/shard_map/sin | solution.py:56
  93.1 42.5 %while.13 = (s32[]{:T(128)}, f32[96,2048]{1,0:T(8,128)}, f32[4,384,96]{2,1,0:T(8,128)}, f32[4,8,2048]{2,1,0:T(8,128)}, f32[4,8,2048]{2,1,0:T(8,128)}, /*index=5*...) while((s32[]{:T(128)}, f32[96,2048]{1,0:T(8,128)}, ...), condition=%wide.region_4.5_spmd.clone.clone.clone, body=%wide.region_3.4_spmd.sunk.clone.clone.clone.sunk | while | flops 911278080 | bytes 17302644 | solution.py:118
  94.0 3.5 %multiply_add_fusion.4 = (f32[8,48,2048]{2,1,0:T(8,128)S(1)}, f32[8,48,2048]{2,1,0:T(8,128)}) fusion(f32[48,2048]{1,0:T(8,128)S(1)} %get-tuple-element.250, f32[8,2048]{1,0:T(8,128)S(1)} %get-tuple-element.219, f32[48,2048]{1,0:T(8,128)} %get-tuple-element.251, f32[8,2048]{1,0:T(8,128)S(1)} %get-tuple-element.220), kind=kLoop, calls=%fused_computation.clone.1 | loop fusion | flops 4718592 | bytes 7208960 | tf_op jit(solution)/shard_map/while/body/eval_jaxpr/add | solution.py:114
  97.5 3.1 %convolution_add_fusion.6 = f32[96,2048]{1,0:T(8,128)S(1)} fusion(f32[384,2048]{1,0:T(8,128)} %bitcast.176, f32[96,2048]{1,0:T(8,128)} %get-tuple-element.234, pred[]{:T(512)S(6)} %compare.5, f32[4,384,96]{2,1,0:T(8,128)} %get-tuple-element.245, s32[]{:T(128)} %get-tuple-element.233), kind=kOutput, calls=%fused_computation.3.clone.1 | convolution fusion | flops 453378048 | bytes 4915713 | tf_op jit(solution)/shard_map/while/body/eval_jaxpr/dot_general | solution.py:29
  100.7 3.0 %convolution_add_fusion.7 = f32[96,2048]{1,0:T(8,128)} fusion(f32[96,2048]{1,0:T(8,128)S(1)} %convolution_add_fusion.6, f32[384,2048]{1,0:T(8,128)S(1)} %bitcast.175, f32[4,384,96]{2,1,0:T(8,128)} %get-tuple-element.248, s32[]{:T(128)} %get-tuple-element.233), kind=kOutput, calls=%fused_computation.2.clone.1 | convolution fusion | flops 453181440 | bytes 4915712 | tf_op jit(solution)/shard_map/while/body/eval_jaxpr/dot_general | solution.py:29
  104.5 3.5 %multiply_add_fusion.4 = (f32[8,48,2048]{2,1,0:T(8,128)S(1)}, f32[8,48,2048]{2,1,0:T(8,128)}) fusion(f32[48,2048]{1,0:T(8,128)S(1)} %get-tuple-element.250, f32[8,2048]{1,0:T(8,128)S(1)} %get-tuple-element.219, f32[48,2048]{1,0:T(8,128)} %get-tuple-element.251, f32[8,2048]{1,0:T(8,128)S(1)} %get-tuple-element.220), kind=kLoop, calls=%fused_computation.clone.1 | loop fusion | flops 4718592 | bytes 7208960 | tf_op jit(solution)/shard_map/while/body/eval_jaxpr/add | solution.py:114
  108.0 3.3 %convolution_add_fusion.6 = f32[96,2048]{1,0:T(8,128)S(1)} fusion(f32[384,2048]{1,0:T(8,128)} %bitcast.176, f32[96,2048]{1,0:T(8,128)} %get-tuple-element.234, pred[]{:T(512)S(6)} %compare.5, f32[4,384,96]{2,1,0:T(8,128)} %get-tuple-element.245, s32[]{:T(128)} %get-tuple-element.233), kind=kOutput, calls=%fused_computation.3.clone.1 | convolution fusion | flops 453378048 | bytes 4915713 | tf_op jit(solution)/shard_map/while/body/eval_jaxpr/dot_general | solution.py:29
  111.3 3.0 %convolution_add_fusion.7 = f32[96,2048]{1,0:T(8,128)} fusion(f32[96,2048]{1,0:T(8,128)S(1)} %convolution_add_fusion.6, f32[384,2048]{1,0:T(8,128)S(1)} %bitcast.175, f32[4,384,96]{2,1,0:T(8,128)} %get-tuple-element.248, s32[]{:T(128)} %get-tuple-element.233), kind=kOutput, calls=%fused_computation.2.clone.1 | convolution fusion | flops 453181440 | bytes 4915712 | tf_op jit(solution)/shard_map/while/body/eval_jaxpr/dot_general | solution.py:29
  115.2 3.5 %multiply_add_fusion.4 = (f32[8,48,2048]{2,1,0:T(8,128)S(1)}, f32[8,48,2048]{2,1,0:T(8,128)}) fusion(f32[48,2048]{1,0:T(8,128)S(1)} %get-tuple-element.250, f32[8,2048]{1,0:T(8,128)S(1)} %get-tuple-element.219, f32[48,2048]{1,0:T(8,128)} %get-tuple-element.251, f32[8,2048]{1,0:T(8,128)S(1)} %get-tuple-element.220), kind=kLoop, calls=%fused_computation.clone.1 | loop fusion | flops 4718592 | bytes 7208960 | tf_op jit(solution)/shard_map/while/body/eval_jaxpr/add | solution.py:114
  118.7 3.3 %convolution_add_fusion.6 = f32[96,2048]{1,0:T(8,128)S(1)} fusion(f32[384,2048]{1,0:T(8,128)} %bitcast.176, f32[96,2048]{1,0:T(8,128)} %get-tuple-element.234, pred[]{:T(512)S(6)} %compare.5, f32[4,384,96]{2,1,0:T(8,128)} %get-tuple-element.245, s32[]{:T(128)} %get-tuple-element.233), kind=kOutput, calls=%fused_computation.3.clone.1 | convolution fusion | flops 453378048 | bytes 4915713 | tf_op jit(solution)/shard_map/while/body/eval_jaxpr/dot_general | solution.py:29
  122.0 3.0 %convolution_add_fusion.7 = f32[96,2048]{1,0:T(8,128)} fusion(f32[96,2048]{1,0:T(8,128)S(1)} %convolution_add_fusion.6, f32[384,2048]{1,0:T(8,128)S(1)} %bitcast.175, f32[4,384,96]{2,1,0:T(8,128)} %get-tuple-element.248, s32[]{:T(128)} %get-tuple-element.233), kind=kOutput, calls=%fused_computation.2.clone.1 | convolution fusion | flops 453181440 | bytes 4915712 | tf_op jit(solution)/shard_map/while/body/eval_jaxpr/dot_general | solution.py:29
  125.8 3.5 %multiply_add_fusion.4 = (f32[8,48,2048]{2,1,0:T(8,128)S(1)}, f32[8,48,2048]{2,1,0:T(8,128)}) fusion(f32[48,2048]{1,0:T(8,128)S(1)} %get-tuple-element.250, f32[8,2048]{1,0:T(8,128)S(1)} %get-tuple-element.219, f32[48,2048]{1,0:T(8,128)} %get-tuple-element.251, f32[8,2048]{1,0:T(8,128)S(1)} %get-tuple-element.220), kind=kLoop, calls=%fused_computation.clone.1 | loop fusion | flops 4718592 | bytes 7208960 | tf_op jit(solution)/shard_map/while/body/eval_jaxpr/add | solution.py:114
  129.4 3.3 %convolution_add_fusion.6 = f32[96,2048]{1,0:T(8,128)S(1)} fusion(f32[384,2048]{1,0:T(8,128)} %bitcast.176, f32[96,2048]{1,0:T(8,128)} %get-tuple-element.234, pred[]{:T(512)S(6)} %compare.5, f32[4,384,96]{2,1,0:T(8,128)} %get-tuple-element.245, s32[]{:T(128)} %get-tuple-element.233), kind=kOutput, calls=%fused_computation.3.clone.1 | convolution fusion | flops 453378048 | bytes 4915713 | tf_op jit(solution)/shard_map/while/body/eval_jaxpr/dot_general | solution.py:29
  132.7 3.0 %convolution_add_fusion.7 = f32[96,2048]{1,0:T(8,128)} fusion(f32[96,2048]{1,0:T(8,128)S(1)} %convolution_add_fusion.6, f32[384,2048]{1,0:T(8,128)S(1)} %bitcast.175, f32[4,384,96]{2,1,0:T(8,128)} %get-tuple-element.248, s32[]{:T(128)} %get-tuple-element.233), kind=kOutput, calls=%fused_computation.2.clone.1 | convolution fusion | flops 453181440 | bytes 4915712 | tf_op jit(solution)/shard_map/while/body/eval_jaxpr/dot_general | solution.py:29
  (53 shorter events, 20.3 us)
Async XLA Ops:
  3.0 1.2 copy-start.2
  4.0 1.8 %copy-start.1 = (f32[2048,96]{1,0:T(8,128)S(1)}, f32[2048,96]{1,0:T(8,128)}, u32[]{:S(2)}) copy-start(f32[2048,96]{1,0:T(8,128)} %constant.86.clone) | copy-start | bytes 2359300
  5.8 2.5 %copy-start.5 = (s32[1,1,2,128]{3,2,1,0:T(2,128)S(1)}, s32[1,1,2,128]{3,2,1,0:T(2,128)}, u32[]{:S(2)}) copy-start(s32[1,1,2,128]{3,2,1,0:T(2,128)} %param.16) | copy-start | bytes 3076
  82.1 3.1 %copy-start.3 = (f32[4,8,2,128]{3,2,1,0:T(2,128)}, f32[4,8,2,128]{3,2,1,0:T(2,128)S(1)}, u32[]{:S(2)}) copy-start(f32[4,8,2,128]{3,2,1,0:T(2,128)S(1)} %psum.7) | copy-start | bytes 98308
  89.5 1.7 %copy-start.4 = (s32[4,8]{1,0:T(4,128)S(1)}, s32[4,8]{1,0:T(4,128)}, u32[]{:S(2)}) copy-start(s32[4,8]{1,0:T(4,128)} %param.15) | copy-start | bytes 388
  89.5 3.6 %copy-start = (f32[48,2048]{1,0:T(8,128)S(1)}, f32[48,2048]{1,0:T(8,128)}, u32[]{:S(2)}) copy-start(f32[48,2048]{1,0:T(8,128)} %constant.173) | copy-start | bytes 1179652
where the time goes:
time: 138 us; the launch traced here: 137 us
  blocking collectives  63.4 us (46%)
  matrix products  39.9 us (29%)
  other arithmetic  20.4 us (15%)
  local copies, waits for them, and re-layouts  12.3 us (9%)
    psum x1, blocking collectives, body(): res = lax.psum(every, ('facet', 'col'))  39.7 us
    dot_general x13, matrix products, dot(): return jnp.dot(a, b, precision=HIGH, preferred_element_type=jnp.float32)  32.7 us
    add x4, other arithmetic, add_column(): cr[:, None, :] * wi.T[None] + ci[:, None, :] * wr.T[None]  14.2 us
    all_gather x1, blocking collectives, body(): uv = lax.all_gather(uv, 'col', axis=0, tiled=True)  13.3 us
    all_gather x1, blocking collectives, body(): uv = lax.all_gather(uv_cells, 'facet', axis=1, tiled=True)  10.4 us
    mul x4, local copies, waits for them, and re-layouts, add_column(): ci[:, None, :] * wi.T[None]  3.52 us
    dot_general x2, matrix products, adot(): jnp.einsum('crsv,lcsv->cslr', a, b, precision=HIGH, preferred_element_typ...  3.11 us
    dot_general x4, matrix products, bdot(): jnp.einsum('skl,lsv->skv', a, b, precision=HIGH, preferred_element_type=j...  2.84 us

commit v1 on v0

--- a/solution.py
+++ b/solution.py
@@ -4,6 +4,8 @@
 import jax.numpy as jnp
 import numpy as np
 from jax import lax
+from jax.experimental import pallas as pl
+from jax.experimental.pallas import tpu as pltpu
 from jax.sharding import PartitionSpec as P
 
 SUBGRID_SIZE = 256
@@ -27,6 +29,177 @@
 
 def dot(a, b):
     return jnp.dot(a, b, precision=HIGH, preferred_element_type=jnp.float32)
+
+
+def split(x):
+    hi = x.astype(jnp.bfloat16)
+    return hi, (x - hi.astype(jnp.float32)).astype(jnp.bfloat16)
+
+
+def dot3(a, b, dims):
+    def one(x, y):
+        return lax.dot_general(x, y, (dims, ((), ())), preferred_element_type=jnp.float32)
+
+    (ah, al), (bh, bl) = split(a), split(b)
+    return one(ah, bh) + (one(ah, bl) + one(al, bh))
+
+
+def exchange_kernel(facets, ncol, add, x_ref, o_ref, slots, held, s1, r1, s2, r2):
+    f = lax.axis_index("facet")
+    c = lax.axis_index("col")
+    mesh_id = pl.DeviceIdType.MESH
+    barrier = pltpu.get_barrier_semaphore()
+    for d in range(1, facets):
+        pl.semaphore_signal(barrier, inc=1, device_id=(lax.rem(f + d, facets), c), device_id_type=mesh_id)
+    for d in range(1, ncol):
+        pl.semaphore_signal(barrier, inc=1, device_id=(f, lax.rem(c + d, ncol)), device_id_type=mesh_id)
+    pl.semaphore_wait(barrier, facets + ncol - 2)
+    copies = []
+    for d in range(1, facets):
+        copies.append(
+            pltpu.make_async_remote_copy(
+                src_ref=x_ref,
+                dst_ref=slots.at[d - 1],
+                send_sem=s1.at[d - 1],
+                recv_sem=r1.at[d - 1],
+                device_id=(lax.rem(f + d, facets), c),
+                device_id_type=mesh_id,
+            )
+        )
+        copies[-1].start()
+    total = x_ref[...]
+    if not add:
+        held[c, f] = total
+    for d in range(1, facets):
+        copies[d - 1].wait_recv()
+        if add:
+            total = total + slots[d - 1]
+        else:
+            held[c, lax.rem(f - d + facets, facets)] = slots[d - 1]
+    if add:
+        held[c] = total
+    later = []
+    for d in range(1, ncol):
+        later.append(
+            pltpu.make_async_remote_copy(
+                src_ref=held.at[c],
+                dst_ref=held.at[c],
+                send_sem=s2.at[d - 1],
+                recv_sem=r2.at[d - 1],
+                device_id=(f, lax.rem(c + d, ncol)),
+                device_id_type=mesh_id,
+            )
+        )
+        later[-1].start()
+    for copy in copies:
+        copy.wait_send()
+    for copy in later:
+        copy.wait()
+    o_ref[...] = held[...]
+
+
+def exchange(x, facets, ncol, add, collective_id):
+    shape = (ncol,) + (x.shape if add else (facets,) + x.shape)
+    return pl.pallas_call(
+        lambda *refs: exchange_kernel(facets, ncol, add, *refs),
+        out_shape=jax.ShapeDtypeStruct(shape, x.dtype),
+        in_specs=[pl.BlockSpec(memory_space=pltpu.VMEM)],
+        out_specs=pl.BlockSpec(memory_space=pltpu.VMEM),
+        scratch_shapes=[
+            pltpu.VMEM((facets - 1,) + x.shape, x.dtype),
+            pltpu.VMEM(shape, x.dtype),
+            pltpu.SemaphoreType.DMA((facets - 1,)),
+            pltpu.SemaphoreType.DMA((facets - 1,)),
+            pltpu.SemaphoreType.DMA((ncol - 1,)),
+            pltpu.SemaphoreType.DMA((ncol - 1,)),
+        ],
+        compiler_params=pltpu.CompilerParams(collective_id=collective_id, has_side_effects=True),
+    )(x)
+
+
+def small_dft(terms):
+    n = len(terms)
+    if n == 1:
+        return terms
+    even, odd = small_dft(terms[::2]), small_dft(terms[1::2])
+    first, second = [], []
+    for j in range(n // 2):
+        (er, ei), (r, i) = even[j], odd[j]
+        if 4 * j == n:
+            r, i = -i, r
+        elif j:
+            a, b = math.cos(2 * math.pi * j / n), math.sin(2 * math.pi * j / n)
+            r, i = r * a - i * b, r * b + i * a
+        first.append((er + r, ei + i))
+        second.append((er - r, ei - i))
+    return first + second
+
+
+def image_kernel(res_ref, pg_ref, gv_ref, place_ref, wave_ref, turn_ref, o_ref, d_ref, grid_ref):
+    ncol, per_col, _, vis = res_ref.shape
+    width = gv_ref.shape[1] // 2
+    length = o_ref.shape[1]
+    lanes = wave_ref.shape[0]
+    grid_ref[...] = jnp.zeros_like(grid_ref)
+
+    def column(c, carry):
+        for s in range(per_col):
+            span = slice(s * vis, (s + 1) * vis)
+            rr, ri = res_ref[c, s, 0:1, :], res_ref[c, s, 1:2, :]
+            pr, pi = pg_ref[c, :width, span], pg_ref[c, width:, span]
+            qr, qi = pr * rr - pi * ri, pr * ri + pi * rr
+            q = jnp.concatenate(
+                [jnp.concatenate([qr, qi], axis=1), jnp.concatenate([qi, -qr], axis=1)], axis=0
+            )
+            g = jnp.concatenate([gv_ref[c, :width, span], gv_ref[c, width:, span]], axis=1)
+            d_ref[s * width : (s + 1) * width, :] = dot3(g, q, ((1,), (1,)))
+        spots = lax.broadcasted_iota(jnp.int32, (per_col * width, length), 1)
+        hot = jnp.where(spots == place_ref[c], 1.0, 0.0).astype(jnp.bfloat16)
+        dims = (((1,), (0,)), ((), ()))
+        for part in split(d_ref[...].T):
+            grid_ref[...] += lax.dot_general(part, hot, dims, preferred_element_type=jnp.float32)
+        return carry
+
+    lax.fori_loop(0, ncol, column, 0)
+    terms = []
+    for rho in range(length // lanes):
+        z = dot3(grid_ref[:, rho * lanes : (rho + 1) * lanes], wave_ref[...], ((1,), (0,)))
+        zr = z[:width, :lanes] - z[width:, lanes:]
+        zi = z[:width, lanes:] + z[width:, :lanes]
+        tr, ti = turn_ref[rho : rho + 1, :lanes], turn_ref[rho : rho + 1, lanes:]
+        terms.append((zr * tr - zi * ti, zr * ti + zi * tr))
+    for j, (r, i) in enumerate(small_dft(terms)):
+        o_ref[:width, j * lanes : (j + 1) * lanes] = r
+        o_ref[width:, j * lanes : (j + 1) * lanes] = i
+
+
+def form_image(res, pg, gv, offsets, width, length):
+    lanes = 128
+    blocks = length // lanes
+    ncol, per_col = offsets.shape
+    n = (offsets[:, :, None] + jnp.arange(width, dtype=jnp.int32)) % length
+    place = ((n % blocks) * lanes + n // blocks).reshape(ncol, per_col * width, 1)
+    k = np.arange(lanes)
+    wave = unit(k[:, None] * k[None, :], lanes) / math.sqrt(length)
+    turn = unit(np.arange(blocks)[:, None] * k[None, :], length)
+    return pl.pallas_call(
+        image_kernel,
+        out_shape=jax.ShapeDtypeStruct((2 * width, length), jnp.float32),
+        in_specs=[pl.BlockSpec(memory_space=pltpu.VMEM)] * 6,
+        out_specs=pl.BlockSpec(memory_space=pltpu.VMEM),
+        scratch_shapes=[
+            pltpu.VMEM((per_col * width, 2 * width), jnp.float32),
+            pltpu.VMEM((2 * width, length), jnp.float32),
+        ],
+        compiler_params=pltpu.CompilerParams(vmem_limit_bytes=48 * 2**20),
+    )(
+        res,
+        pg,
+        gv,
+        place,
+        jnp.asarray(np.concatenate([wave.real, wave.imag], axis=1).astype(np.float32)),
+        jnp.asarray(np.concatenate([turn.real, turn.imag], axis=1).astype(np.float32)),
+    )
 
 
 def body(strips, sub_offset, uv_cells, measured):
@@ -40,24 +213,26 @@
     rows_all = width * ncol
     xr, xi = strips[0, 0], strips[0, 1]
 
-    uv = lax.all_gather(uv_cells, "facet", axis=1, tiled=True)
-    uv = lax.all_gather(uv, "col", axis=0, tiled=True)
+    uv = exchange(uv_cells[0], facets, ncol, False, 1).reshape(ncol, per_col, 2, vis)
     h = lax.dynamic_index_in_dim(jnp.asarray(pick_table(facets, width)), f, 0, keepdims=False)
     cells = jnp.arange(SUBGRID_SIZE, dtype=jnp.int32)[:, None]
     pick_u = (cells == uv[:, :, 0].reshape(1, -1)).astype(jnp.float32)
     pick_v = (cells == uv[:, :, 1].reshape(1, -1)).astype(jnp.float32)
-    gv = dot(h, pick_v).reshape(2, width, ncol, per_col, vis)
+    gv = jnp.einsum(
+        "ku,ucx->ckx", h, pick_v.reshape(SUBGRID_SIZE, ncol, per_col * vis),
+        precision=HIGH, preferred_element_type=jnp.float32,
+    )
     own_u = lax.dynamic_slice_in_dim(pick_u, c * per_col * vis, per_col * vis, 1)
     gu = dot(h, own_u).reshape(2, width, per_col, vis)
-    own_v = lax.dynamic_index_in_dim(gv, c, 2, keepdims=False)
+    own_v = lax.dynamic_index_in_dim(gv, c, 0, keepdims=False).reshape(2, width, per_col, vis)
 
     j = jnp.arange(length, dtype=jnp.int32)
-    ang = ((sub_offset.reshape(-1, 1) * j[None, :]) % length).astype(jnp.float32) * (2.0 * math.pi / length)
+    own = lax.dynamic_index_in_dim(sub_offset, c, 0, keepdims=False)
+    ang = ((own[:, None] * j[None, :]) % length).astype(jnp.float32) * (2.0 * math.pi / length)
     pr, pi = jnp.cos(ang), jnp.sin(ang)
     w = unit(np.arange(length)[:, None] * np.arange(width)[None, :], length) / math.sqrt(length)
     wr, wi = np.real(w).astype(np.float32), np.imag(w).astype(np.float32)
-    opr = lax.dynamic_slice_in_dim(pr, c * per_col, per_col, 0)[:, None, :]
-    opi = lax.dynamic_slice_in_dim(pi, c * per_col, per_col, 0)[:, None, :]
+    opr, opi = pr[:, None, :], pi[:, None, :]
     sr = (xr[None] * opr + xi[None] * opi).reshape(per_col * width, length)
     si = (xi[None] * opr - xr[None] * opi).reshape(per_col * width, length)
     wide = np.concatenate([wr, -wi], axis=1), np.concatenate([wi, wr], axis=1)
@@ -77,9 +252,7 @@
     per_dev = measured.shape[1]
     mine = lax.dynamic_slice_in_dim(part, f * per_dev, per_dev, 0) + measured[0]
     part = lax.dynamic_update_slice_in_dim(part, mine, f * per_dev, 0)
-    every = jnp.zeros((ncol,) + part.shape, jnp.float32)
-    every = lax.dynamic_update_slice_in_dim(every, part[None], c, 0)
-    res = lax.psum(every, ("facet", "col"))
+    res = exchange(part, facets, ncol, True, 2)
     residual_vis = lax.dynamic_slice(res, (c, f * per_dev, 0, 0), (1, per_dev, 2, vis))
 
     r = np.arange(rows_all)
@@ -93,33 +266,8 @@
     pg = jnp.einsum(
         "cru,ucx->crx", ph, pick_u.reshape(SUBGRID_SIZE, ncol, per_col * vis),
         precision=HIGH, preferred_element_type=jnp.float32,
-    ).reshape(ncol, 2, width, per_col, vis)
-    rr, ri = res[:, None, :, 0], res[:, None, :, 1]
-    qr = pg[:, 0] * rr - pg[:, 1] * ri
-    qi = pg[:, 0] * ri + pg[:, 1] * rr
-    q = jnp.concatenate([qr, qi], axis=1)
-
-    def adot(a, b):
-        return jnp.einsum("crsv,lcsv->cslr", a, b, precision=HIGH, preferred_element_type=jnp.float32)
-
-    dgr, dgi = adot(q, gv[0]), adot(q, gv[1])
-    dr = dgr[..., :width] + dgi[..., width:]
-    di = dgr[..., width:] - dgi[..., :width]
-    left = jnp.concatenate([dr, di], -1).reshape(ncol, -1, 2 * width)
-    right = jnp.concatenate([-di, dr], -1).reshape(ncol, -1, 2 * width)
-
-    def add_column(acc, item):
-        l, r, cr, ci = item
-        vr = (cr[:, None, :] * wr.T[None] - ci[:, None, :] * wi.T[None]).reshape(-1, length)
-        vi = (cr[:, None, :] * wi.T[None] + ci[:, None, :] * wr.T[None]).reshape(-1, length)
-        return acc + dot(l.T, vr) + dot(r.T, vi), None
-
-    shape = (ncol, per_col, length)
-    image, _ = lax.scan(
-        add_column,
-        jnp.zeros((2 * width, length), jnp.float32),
-        (left, right, pr.reshape(shape), pi.reshape(shape)),
-    )
+    )
+    image = form_image(res, pg, gv, sub_offset, width, length)
     return image.reshape(1, 2, width, length), residual_vis
 
 

time: 138 us -> 52.9 us (0.38)
  blocking collectives: 63.4 us -> 0 us
  Pallas kernels: 0 us -> 31.6 us
  matrix products: 39.9 us -> 10.2 us
  other arithmetic: 20.4 us -> 3.5 us
  local copies, waits for them, and re-layouts: 12.3 us -> 6.14 us
    psum x1 -> x0, blocking collectives: 39.7 us -> none  [body(): res = lax.psum(every, ('facet', 'col'))]
    pallas_call x0 -> x3, Pallas kernels: none -> 31.6 us  [the longest x2 23.8 us: exchange(): pl.pallas_call(lambda *refs: exchange_kernel(facets, ncol, add, *refs), o...]
    dot_general x13 -> x4, matrix products: 32.7 us -> 5.75 us  [dot(): return jnp.dot(a, b, precision=HIGH, preferred_element_type=jnp.float32)]
    all_gather x2 -> x0, blocking collectives: 23.7 us -> none  [the longest x1 13.3 us: body(): uv = lax.all_gather(uv, 'col', axis=0, tiled=True)]
    add x4 -> x1, other arithmetic: 14.2 us -> 2.22 us  [form_image(): place = (n % blocks * lanes + n // blocks).reshape(ncol, per_col * width, 1)]
    mul x5 -> x1, local copies, waits for them, and re-layouts: 4.29 us -> 0.69 us  [body(): own[:, None] * j[None, :]]
    sin x1 -> x0, other arithmetic: 1.91 us -> none  [body(): pr, pi = (jnp.cos(ang), jnp.sin(ang))]
    dot_general x4, matrix products: 2.84 us -> 1 us  [bdot(): jnp.einsum('skl,lsv->skv', a, b, precision=HIGH, preferred_element_type=j...]
where the time goes in v1:
time: 52.9 us; the launch traced here: 52.5 us
  Pallas kernels  31.6 us (60%)
  matrix products  10.2 us (19%)
  local copies, waits for them, and re-layouts  6.14 us (12%)
  other arithmetic  3.5 us (7%)
  between operations  0.95 us (2%)
    pallas_call x2, Pallas kernels, exchange(): pl.pallas_call(lambda *refs: exchange_kernel(facets, ncol, add, *refs), o...  23.8 us
    pallas_call x1, Pallas kernels, form_image(): pl.pallas_call(image_kernel, out_shape=jax.ShapeDtypeStruct((2 * width, l...  7.78 us
    dot_general x4, matrix products, dot(): return jnp.dot(a, b, precision=HIGH, preferred_element_type=jnp.float32)  5.75 us
    dot_general x1, matrix products, body(): jnp.einsum('ku,ucx->ckx', h, pick_v.reshape(SUBGRID_SIZE, ncol, per_col *...  2.24 us
    add x1, other arithmetic, form_image(): place = (n % blocks * lanes + n // blocks).reshape(ncol, per_col * width, 1)  2.22 us
    add x4, local copies, waits for them, and re-layouts, form_image(): n = (offsets[:, :, None] + jnp.arange(width, dtype=jnp.int32)) % length  1.43 us
    dot_general x1, matrix products, body(): jnp.einsum('cru,ucx->crx', ph, pick_u.reshape(SUBGRID_SIZE, ncol, per_col...  1.25 us
    mul x1, local copies, waits for them, and re-layouts, body(): sr = (xr[None] * opr + xi[None] * opi).reshape(per_col * width, length)  1.17 us

profile of v1, /device:TPU:0, one launch (start us, length us, event | category | flops | bytes accessed | tf_op | source)
XLA Modules:
  0.0 52.5 jit_solution(8445207829904295148)
XLA Ops:
  0.6 0.7 %fusion.44 = s32[8]{0:T(128)S(1)} fusion(s32[4,8]{1,0:T(4,128)} %param.11, s32[]{:T(128)S(6)} %select_n.69), kind=kLoop, calls=%fused_computation.84 | loop fusion | bytes 68 | tf_op jit(solution)/shard_map/mul | solution.py:231
  1.3 0.3 fusion.39
  1.7 1.2 %slice_bitcast_fusion.1 = (f32[48,2048]{1,0:T(8,128)S(1)}, f32[48,2048]{1,0:T(8,128)S(1)}) fusion(f32[1,2,48,2048]{3,2,1,0:T(8,128)} %param.10), kind=kLoop, calls=%fused_computation.33 | loop fusion | bytes 1572864 | tf_op jit(solution)/shard_map/mul | solution.py:236
  2.9 0.9 %multiply_subtract_fusion = (f32[8,48,2048]{2,1,0:T(8,128)S(1)}, f32[8,48,2048]{2,1,0:T(8,128)S(1)}) fusion(f32[8,2048]{1,0:T(8,128)S(1)} %get-tuple-element.18, f32[48,2048]{1,0:T(8,128)S(1)} %get-tuple-element.9, f32[8,2048]{1,0:T(8,128)S(1)} %get-tuple-element.17, f32[48,2048]{1,0:T(8,128)S(1)} %get-tuple-element.8), kind=kLoop, calls=%fused_computation.5 | loop fusion | flops 4718592 | bytes 7208960 | tf_op jit(solution)/shard_map/sub | solution.py:237
  3.8 0.3 copy-done.4
  4.1 1.5 %fusion.46 = f32[384,96]{0,1:T(8,128)S(1)} fusion(f32[384,2048]{1,0:T(8,128)S(1)} %bitcast.115, f32[2048,96]{1,0:T(8,128)S(1)} %copy-done.4), kind=kOutput, calls=%fused_computation.87 | convolution fusion | flops 452984832 | bytes 4079616 | tf_op jit(solution)/shard_map/dot_general | solution.py:31
  5.6 1.6 %convolution_add_fusion.1 = f32[384,96]{0,1:T(8,128)S(1)} fusion(f32[384,96]{0,1:T(8,128)S(1)} %fusion.46, f32[384,2048]{1,0:T(8,128)S(1)} %bitcast.114, f32[2048,96]{1,0:T(8,128)S(1)} %copy-done.3), kind=kOutput, calls=%fused_computation.19 | convolution fusion | flops 453021696 | bytes 4227072 | tf_op jit(solution)/shard_map/dot_general | solution.py:31
  7.2 0.1 copy.33
  7.4 12.9 %shard_map.113 = s32[4,8,1,2,128]{4,3,2,1,0:T(2,128)} custom-call(s32[1,2,128]{2,1,0:T(2,128)} %bitcast.133), custom_call_target="tpu_custom_call" | custom-call | tf_op jit(solution)/shard_map/pallas_call | solution.py:103
  20.3 0.9 %slice_reduce_fusion.1 = (s32[4,8,128]{2,1,0:T(8,128)S(1)}, s32[4,8,128]{2,1,0:T(8,128)S(1)}, s32[4,8,1,128]{3,2,1,0:T(1,128)S(1)}) fusion(s32[4,8,2,128]{3,2,1,0:T(2,128)} %bitcast.125), kind=kLoop, calls=%fused_computation.85 | loop fusion | bytes 81920 | tf_op jit(solution)/shard_map/slice | solution.py:219
  21.2 2.2 %fusion.1 = f32[4,1024,96]{1,2,0:T(8,128)S(1)} fusion(s32[4,1024]{1,0:T(4,128)S(1)} %bitcast.127, f32[8,96,256]{2,1,0:T(8,128)} %constant.103.clone, s32[]{:T(128)S(6)} %select_n.71), kind=kOutput, calls=%fused_computation.3 | convolution fusion | flops 605028352 | bytes 1687556 | tf_op jit(solution)/shard_map/ku,ucx->ckx/dot_general | solution.py:221
  23.6 0.2 fusion.30
  24.0 0.2 convolution_subtract_fusion
  24.3 0.2 fusion.26
  24.5 1.3 %fusion.6 = f32[96,1024]{1,0:T(8,128)S(1)} fusion(s32[1024]{0:T(1024)S(1)} %dynamic-slice.4, f32[8,96,256]{2,1,0:T(8,128)} %constant.103.clone, s32[]{:T(128)S(6)} %select_n.71), kind=kOutput, calls=%fused_computation.21 | convolution fusion | flops 151257088 | bytes 495620 | tf_op jit(solution)/shard_map/dot_general | solution.py:31
  25.9 0.3 fusion.18
  26.3 0.6 %copy-done.5 = f32[8,2,128]{2,1,0:T(2,128)} copy-done((f32[8,2,128]{2,1,0:T(2,128)}, f32[8,2,128]{2,1,0:T(2,128)S(1)}, u32[]{:S(2)}) %copy-start.5) | copy-done | bytes 8216
  26.9 10.9 %shard_map.114.res_ref = f32[4,8,2,128]{3,2,1,0:T(2,128)} custom-call(f32[8,2,128]{2,1,0:T(2,128)} %copy-done.5), custom_call_target="tpu_custom_call" | custom-call | tf_op jit(solution)/shard_map/pallas_call | solution.py:103
  37.8 1.3 %fusion.23 = f32[4,96,256]{2,1,0:T(8,128)S(1)} fusion(f32[4,4,96,96]{3,2,1,0:T(8,128)} %constant.106.clone, s32[]{:T(128)S(6)} %select_n.69, f32[8,96,256]{2,1,0:T(8,128)} %constant.103.clone, s32[]{:T(128)S(6)} %select_n.71), kind=kOutput, calls=%fused_computation.48 | convolution fusion | flops 56623104 | bytes 688136 | tf_op jit(solution)/shard_map/dot_general | solution.py:31
  39.2 1.3 %fusion.3.pg_ref = f32[4,96,1024]{2,1,0:T(8,128)S(1)} fusion(f32[4,96,256]{2,1,0:T(8,128)S(1)} %fusion.23, s32[4,1024]{1,0:T(4,128)S(1)} %bitcast.126), kind=kOutput, calls=%fused_computation.4 | convolution fusion | flops 605028352 | bytes 1982464 | tf_op jit(solution)/shard_map/cru,ucx->crx/dot_general | solution.py:266
  40.5 1.3 %add.138 = s32[4,384,1]{2,1,0:T(8,128)} reshape(s32[4,8,48]{2,1,0:T(8,128)S(1)} %add.129) | data formatting | bytes 12288 | tf_op jit(solution)/shard_map/add | solution.py:180
  41.9 2.2 %fusion.9.place_ref = s32[4,384,1]{2,1,0:T(8,128)S(1)} fusion(s32[4,384,1]{2,1,0:T(8,128)} %add.138, s32[384]{0:T(512)S(1)} %add.132), kind=kLoop, calls=%fused_computation.24 | loop fusion | flops 50688 | bytes 13824 | tf_op jit(solution)/shard_map/add | solution.py:181
  44.1 7.8 %shard_map.115 = f32[96,2048]{1,0:T(8,128)} custom-call(f32[4,8,2,128]{3,2,1,0:T(2,128)S(1)} %copy-done, f32[4,96,1024]{2,1,0:T(8,128)S(1)} %fusion.3.pg_ref, f32[4,96,1024]{2,1,0:T(8,128)S(1)} %bitcast.113, s32[4,384,1]{2,1,0:T(8,128)S(1)} %fusion.9.place_ref, f32[128,256]{1,0:T(8,128)S(1)} %copy-done.1, f32[16,256]{1,0:T(8,128)S(1)} %copy-done.2), custom_call_target="tpu_custom_call" | custom-call | tf_op jit(solution)/shard_map/pallas_call | solution.py:185
  51.9 0.6 %constant_dynamic-slice_fusion.1 = f32[1,1,2,128]{3,2,1,0:T(2,128)} fusion(f32[4,8,2,128]{3,2,1,0:T(2,128)S(1)} %copy-done, s32[]{:T(128)S(6)} %select_n.69, s32[]{:T(128)S(6)} %select_n.71), kind=kLoop, calls=%fused_computation.80 | loop fusion | bytes 2056 | tf_op jit(solution)/shard_map/dynamic_slice | solution.py:256
  (30 shorter events, 0.6 us)
Async XLA Ops:
  2.8 1.2 %copy-start.4 = (f32[2048,96]{1,0:T(8,128)S(1)}, f32[2048,96]{1,0:T(8,128)}, u32[]{:S(2)}) copy-start(f32[2048,96]{1,0:T(8,128)} %constant.104.clone) | copy-start | bytes 2359300
  3.8 1.8 %copy-start.3 = (f32[2048,96]{1,0:T(8,128)S(1)}, f32[2048,96]{1,0:T(8,128)}, u32[]{:S(2)}) copy-start(f32[2048,96]{1,0:T(8,128)} %constant.105.clone) | copy-start | bytes 2359300
  23.5 2.7 %copy-start.7 = (f32[1,1,2,128]{3,2,1,0:T(2,128)S(1)}, f32[1,1,2,128]{3,2,1,0:T(2,128)}, u32[]{:S(2)}) copy-start(f32[1,1,2,128]{3,2,1,0:T(2,128)} %param.13) | copy-start | bytes 3076
  24.0 16.4 %copy-start.6 = (s32[4,8]{1,0:T(4,128)S(1)}, s32[4,8]{1,0:T(4,128)}, u32[]{:S(2)}) copy-start(s32[4,8]{1,0:T(4,128)} %param.11) | copy-start | bytes 388
  25.9 18.2 %copy-start.1 = (f32[128,256]{1,0:T(8,128)S(1)}, f32[128,256]{1,0:T(8,128)}, u32[]{:S(2)}) copy-start(f32[128,256]{1,0:T(8,128)} %constant.107.clone.wave_ref) | copy-start | bytes 393220
  25.9 18.2 %copy-start.2 = (f32[16,256]{1,0:T(8,128)S(1)}, f32[16,256]{1,0:T(8,128)}, u32[]{:S(2)}) copy-start(f32[16,256]{1,0:T(8,128)} %constant.108.clone.turn_ref) | copy-start | bytes 49156
  26.3 0.6 %copy-start.5 = (f32[8,2,128]{2,1,0:T(2,128)}, f32[8,2,128]{2,1,0:T(2,128)S(1)}, u32[]{:S(2)}) copy-start(f32[8,2,128]{2,1,0:T(2,128)S(1)} %constant_dynamic-update-slice_fusion.refs_0_) | copy-start | bytes 24580
  37.8 6.3 %copy-start = (f32[4,8,2,128]{3,2,1,0:T(2,128)S(1)}, f32[4,8,2,128]{3,2,1,0:T(2,128)}, u32[]{:S(2)}) copy-start(f32[4,8,2,128]{3,2,1,0:T(2,128)} %shard_map.114.res_ref) | copy-start | bytes 98308

commit v2 on v1

v2 whole, which is shorter than its diff:
```python
import math

import jax
import jax.numpy as jnp
import numpy as np
from jax import lax
from jax.experimental import pallas as pl
from jax.experimental.pallas import tpu as pltpu
from jax.sharding import PartitionSpec as P

SUBGRID_SIZE = 256
HIGH = lax.Precision.HIGH


def unit(numer, denom):
    angle = (np.asarray(numer) % denom) * (2.0 * math.pi / denom)
    return np.exp(1j * angle)


def pick_table(facets, width):
    total = facets * width
    cells = np.arange(SUBGRID_SIZE)
    factor = (facets * width * width) ** -0.25
    e = factor * unit(np.arange(total)[:, None] * cells[None, :], total)
    h = e @ unit(-cells[:, None] * cells[None, :], SUBGRID_SIZE)
    h = h.reshape(facets, width, SUBGRID_SIZE)
    return np.concatenate([h.real, h.imag], axis=1).astype(np.float32)


def dot(a, b):
    return jnp.dot(a, b, precision=HIGH, preferred_element_type=jnp.float32)


def split(x):
    hi = x.astype(jnp.bfloat16)
    return hi, (x - hi.astype(jnp.float32)).astype(jnp.bfloat16)


def dot3(a, b, dims):
    def one(x, y):
        return lax.dot_general(x, y, (dims, ((), ())), preferred_element_type=jnp.float32)

    (ah, al), (bh, bl) = split(a), split(b)
    return one(ah, bh) + (one(ah, bl) + one(al, bh))


def placed(offsets, width, length, lanes):
    blocks = length // lanes
    steps = lax.broadcasted_iota(jnp.int32, (width, 1), 0)
    cells = [(offsets[s : s + 1, :] + steps) & (length - 1) for s in range(offsets.shape[0])]
    n = jnp.concatenate(cells, axis=0)
    spot = (n & (blocks - 1)) * lanes + (n >> (blocks.bit_length() - 1))
    spots = lax.broadcasted_iota(jnp.int32, (n.shape[0], length), 1)
    return jnp.where(spots == spot, 1.0, 0.0).astype(jnp.bfloat16)


def picked(parts, index):
    cells = lax.broadcasted_iota(jnp.int32, (SUBGRID_SIZE, index.shape[1]), 0)
    hot = jnp.where(cells == index, 1.0, 0.0).astype(jnp.bfloat16)
    dims = (((1,), (0,)), ((), ()))
    high, low = [lax.dot_general(p, hot, dims, preferred_element_type=jnp.float32) for p in parts]
    return high + low


def predict_kernel(
    facets, ncol, x_ref, uv_ref, meas_ref, off_ref, h_ref, wave_ref, turn_ref,
    res_ref, all_uv_ref, own_ref,
    uv_slots, uv_held, part_ref, slots, held, grid_ref, kt_ref, s1, r1, s2, r2, s3, r3, s4, r4,
):
    f = lax.axis_index("facet")
    c = lax.axis_index("col")
    mesh_id = pl.DeviceIdType.MESH
    width, length = x_ref.shape[1], x_ref.shape[2]
    lanes = wave_ref.shape[0]
    blocks = length // lanes

    def over_facets(src, dst, send, recv):
        copies = [
            pltpu.make_async_remote_copy(
                src_ref=src,
                dst_ref=dst.at[d - 1],
                send_sem=send.at[d - 1],
                recv_sem=recv.at[d - 1],
                device_id=(lax.rem(f + d, facets), c),
                device_id_type=mesh_id,
            )
            for d in range(1, facets)
        ]
        for copy in copies:
            copy.start()
        return copies

    def over_columns(ref, send, recv):
        copies = [
            pltpu.make_async_remote_copy(
                src_ref=ref.at[c],
                dst_ref=ref.at[c],
                send_sem=send.at[d - 1],
                recv_sem=recv.at[d - 1],
                device_id=(f, lax.rem(c + d, ncol)),
                device_id_type=mesh_id,
            )
            for d in range(1, ncol)
        ]
        for copy in copies:
            copy.start()
        return copies

    barrier = pltpu.get_barrier_semaphore()
    for d in range(1, facets):
        pl.semaphore_signal(barrier, inc=1, device_id=(lax.rem(f + d, facets), c), device_id_type=mesh_id)
    for d in range(1, ncol):
        pl.semaphore_signal(barrier, inc=1, device_id=(f, lax.rem(c + d, ncol)), device_id_type=mesh_id)
    pl.semaphore_wait(barrier, facets + ncol - 2)
    uv_copies = over_facets(uv_ref, uv_slots, s1, r1)

    spans = [slice(i * lanes, (i + 1) * lanes) for i in range(blocks)]
    for rho, (yr, yi) in enumerate(small_dft([(x_ref[0, :, i], -x_ref[1, :, i]) for i in spans])):
        tr, ti = turn_ref[rho : rho + 1, :lanes], turn_ref[rho : rho + 1, lanes:]
        z = jnp.concatenate([yr * tr - yi * ti, yr * ti + yi * tr], axis=0)
        p = dot3(z, wave_ref[...], ((1,), (0,)))
        grid_ref[:width, spans[rho]] = p[:width, :lanes] - p[width:, lanes:]
        grid_ref[width:, spans[rho]] = -(p[:width, lanes:] + p[width:, :lanes])
    hot = placed(off_ref[c], width, length, lanes)
    dims = (((1,), (1,)), ((), ()))
    high, low = [
        lax.dot_general(hot, part, dims, preferred_element_type=jnp.float32)
        for part in split(grid_ref[...])
    ]
    kt_ref[...] = high + low

    uv_held[c, f] = uv_ref[...]
    for d in range(1, facets):
        uv_copies[d - 1].wait_recv()
        uv_held[c, lax.rem(f - d + facets, facets)] = uv_slots[d - 1]
    uv_later = over_columns(uv_held, s2, r2)

    parts = split(h_ref[f])
    for s in range(facets):
        gu = picked(parts, uv_held[c, s, 0:1, :])
        gv = picked(parts, uv_held[c, s, 1:2, :])
        gur, gui, gvr, gvi = gu[:width], gu[width:], gv[:width], gv[width:]
        wide = jnp.concatenate(
            [jnp.concatenate([gur, gui], axis=1), jnp.concatenate([-gui, gur], axis=1)], axis=0
        )
        a = dot3(kt_ref[s * width : (s + 1) * width, :], wide, ((1,), (0,)))
        vis = gu.shape[1]
        ar, ai = a[:, :vis], a[:, vis:]
        pr = jnp.sum(ar * gvr - ai * gvi, axis=0, keepdims=True)
        pi = jnp.sum(ar * gvi + ai * gvr, axis=0, keepdims=True)
        pred = jnp.concatenate([pr, pi], axis=0) * (1.0 / SUBGRID_SIZE)
        part_ref[s] = jnp.where(f == s, meas_ref[...], 0.0) - pred

    copies = over_facets(part_ref, slots, s3, r3)
    total = part_ref[...]
    for d in range(1, facets):
        copies[d - 1].wait_recv()
        total = total + slots[d - 1]
    held[c] = total
    later = over_columns(held, s4, r4)
    own_ref[...] = held[c, f]
    for copy in uv_copies + copies:
        copy.wait_send()
    for copy in uv_later:
        copy.wait()
    all_uv_ref[...] = uv_held[...]
    for copy in later:
        copy.wait()
    res_ref[...] = held[...]


def predict(x, uv, measured, offsets, h, wave, turn, facets, ncol):
    width, length = x.shape[1:]
    pair = uv.shape
    full = (ncol, facets) + pair
    dma = pltpu.SemaphoreType.DMA
    return pl.pallas_call(
        lambda *refs: predict_kernel(facets, ncol, *refs),
        out_shape=(
            jax.ShapeDtypeStruct(full, jnp.float32),
            jax.ShapeDtypeStruct(full, jnp.int32),
            jax.ShapeDtypeStruct(pair, jnp.float32),
        ),
        in_specs=[pl.BlockSpec(memory_space=pltpu.VMEM)] * 7,
        out_specs=[pl.BlockSpec(memory_space=pltpu.VMEM)] * 3,
        scratch_shapes=[
            pltpu.VMEM((facets - 1,) + pair, jnp.int32),
            pltpu.VMEM(full, jnp.int32),
            pltpu.VMEM((facets,) + pair, jnp.float32),
            pltpu.VMEM((facets - 1, facets) + pair, jnp.float32),
            pltpu.VMEM(full, jnp.float32),
            pltpu.VMEM((2 * width, length), jnp.float32),
            pltpu.VMEM((facets * width, 2 * width), jnp.float32),
        ]
        + [dma((facets - 1,))] * 2
        + [dma((ncol - 1,))] * 2
        + [dma((facets - 1,))] * 2
        + [dma((ncol - 1,))] * 2,
        compiler_params=pltpu.CompilerParams(
            collective_id=1, has_side_effects=True, vmem_limit_bytes=48 * 2**20
        ),
    )(x, uv, measured, offsets, h, wave, turn)


def small_dft(terms):
    n = len(terms)
    if n == 1:
        return terms
    even, odd = small_dft(terms[::2]), small_dft(terms[1::2])
    first, second = [], []
    for j in range(n // 2):
        (er, ei), (r, i) = even[j], odd[j]
        if 4 * j == n:
            r, i = -i, r
        elif j:
            a, b = math.cos(2 * math.pi * j / n), math.sin(2 * math.pi * j / n)
            r, i = r * a - i * b, r * b + i * a
        first.append((er + r, ei + i))
        second.append((er - r, ei - i))
    return first + second


def image_kernel(res_ref, uv_ref, off_ref, h_ref, pm_ref, wave_ref, turn_ref, o_ref, d_ref, grid_ref):
    ncol, per_col = res_ref.shape[:2]
    width = h_ref.shape[1] // 2
    h = h_ref[lax.axis_index("facet")]
    rows = lax.axis_index("col")
    parts = split(h)
    length = o_ref.shape[1]
    lanes = wave_ref.shape[0]
    grid_ref[...] = jnp.zeros_like(grid_ref)

    def column(c, carry):
        phase = split(dot3(pm_ref[rows, c], h, ((1,), (0,))))
        for s in range(per_col):
            pg = picked(phase, uv_ref[c, s, 0:1, :])
            gv = picked(parts, uv_ref[c, s, 1:2, :])
            rr, ri = res_ref[c, s, 0:1, :], res_ref[c, s, 1:2, :]
            pr, pi = pg[:width], pg[width:]
            qr, qi = pr * rr - pi * ri, pr * ri + pi * rr
            q = jnp.concatenate(
                [jnp.concatenate([qr, qi], axis=1), jnp.concatenate([qi, -qr], axis=1)], axis=0
            )
            g = jnp.concatenate([gv[:width], gv[width:]], axis=1)
            d_ref[s * width : (s + 1) * width, :] = dot3(g, q, ((1,), (1,)))
        hot = placed(off_ref[c], width, length, lanes)
        dims = (((1,), (0,)), ((), ()))
        for part in split(d_ref[...].T):
            grid_ref[...] += lax.dot_general(part, hot, dims, preferred_element_type=jnp.float32)
        return carry

    lax.fori_loop(0, ncol, column, 0)
    terms = []
    for rho in range(length // lanes):
        z = dot3(grid_ref[:, rho * lanes : (rho + 1) * lanes], wave_ref[...], ((1,), (0,)))
        zr = z[:width, :lanes] - z[width:, lanes:]
        zi = z[:width, lanes:] + z[width:, :lanes]
        tr, ti = turn_ref[rho : rho + 1, :lanes], turn_ref[rho : rho + 1, lanes:]
        terms.append((zr * tr - zi * ti, zr * ti + zi * tr))
    for j, (r, i) in enumerate(small_dft(terms)):
        o_ref[:width, j * lanes : (j + 1) * lanes] = r
        o_ref[width:, j * lanes : (j + 1) * lanes] = i


def form_image(res, uv, offsets, h, pm, wave, turn, width, length):
    per_col = offsets.shape[1]
    return pl.pallas_call(
        image_kernel,
        out_shape=jax.ShapeDtypeStruct((2 * width, length), jnp.float32),
        in_specs=[pl.BlockSpec(memory_space=pltpu.VMEM)] * 7,
        out_specs=pl.BlockSpec(memory_space=pltpu.VMEM),
        scratch_shapes=[
            pltpu.VMEM((per_col * width, 2 * width), jnp.float32),
            pltpu.VMEM((2 * width, length), jnp.float32),
        ],
        compiler_params=pltpu.CompilerParams(vmem_limit_bytes=48 * 2**20),
    )(res, uv, offsets, h, pm, wave, turn)


def sides(z, axis):
    return jnp.asarray(np.concatenate([z.real, z.imag], axis=axis).astype(np.float32))


def body(strips, sub_offset, uv_cells, measured):
    facets = lax.axis_size("facet")
    ncol = lax.axis_size("col")
    width, length = strips.shape[2], strips.shape[3]
    assert uv_cells.shape[1] == 1 and sub_offset.shape[1] == facets
    rows_all = width * ncol
    lanes = 128
    k = np.arange(lanes)
    wave = sides(unit(k[:, None] * k[None, :], lanes) / math.sqrt(length), 1)
    turn = sides(unit(np.arange(length // lanes)[:, None] * k[None, :], length), 1)
    h = jnp.asarray(pick_table(facets, width))
    r = np.arange(rows_all)
    p = unit(r[:, None] * r[None, :], rows_all) / math.sqrt(rows_all)
    p = p.reshape(ncol, width, ncol, width).transpose(0, 2, 1, 3)
    pm = np.concatenate(
        [
            np.concatenate([p.real, p.imag], axis=3),
            np.concatenate([p.imag, -p.real], axis=3),
        ],
        axis=2,
    ).astype(np.float32)
    offsets = sub_offset[:, :, None]
    res, uv, own = predict(
        strips[0], uv_cells[0, 0], measured[0, 0], offsets, h, wave, turn, facets, ncol
    )
    image = form_image(res, uv, offsets, h, jnp.asarray(pm), wave, turn, width, length)
    return image.reshape(1, 2, width, length), own[None, None]


def solution(mesh):
    return jax.shard_map(
        body,
        mesh=mesh,
        in_specs=(
            P("facet", None, "col", None),
            P(),
            P("col", "facet", None, None),
            P("col", "facet", None, None),
        ),
        out_specs=(P("facet", None, "col", None), P("col", "facet", None, None)),
        check_vma=False,
    )
```

time: 52.9 us -> 36.7 us (0.69)
  matrix products: 10.2 us -> 0 us
  other arithmetic: 3.5 us -> 0 us
  local copies, waits for them, and re-layouts: 6.14 us -> 4.54 us
    dot_general x10 -> x0, matrix products: 10.2 us -> none  [the longest x4 5.75 us: dot(): return jnp.dot(a, b, precision=HIGH, preferred_element_type=jnp.float32)]
    pallas_call x2 -> x1, Pallas kernels: 23.8 us -> 17.5 us  [predict(): pl.pallas_call(lambda *refs: predict_kernel(facets, ncol, *refs), out_sha...]
    pallas_call x1, Pallas kernels: 7.78 us -> 13.7 us  [form_image(): pl.pallas_call(image_kernel, out_shape=jax.ShapeDtypeStruct((2 * width, l...]
    unnamed x22 -> x17, local copies, waits for them, and re-layouts: 1.07 us -> 3.75 us
    add x1 -> x0, other arithmetic: 2.22 us -> none  [form_image(): place = (n % blocks * lanes + n // blocks).reshape(ncol, per_col * width, 1)]
    mul x2 -> x0, local copies, waits for them, and re-layouts: 1.86 us -> none  [the longest x1 1.17 us: body(): sr = (xr[None] * opr + xi[None] * opi).reshape(per_col * width, length)]
    add x4 -> x0, local copies, waits for them, and re-layouts: 1.43 us -> none  [form_image(): n = (offsets[:, :, None] + jnp.arange(width, dtype=jnp.int32)) % length]
    slice x2 -> x0, local copies, waits for them, and re-layouts: 0.94 us -> none  [the longest x1 0.93 us: body(): pick_u = (cells == uv[:, :, 0].reshape(1, -1)).astype(jnp.float32)]
where the time goes in v2:
time: 36.7 us; the launch traced here: 36.5 us
  Pallas kernels  31.2 us (85%)
  local copies, waits for them, and re-layouts  4.54 us (12%)
  between operations  0.69 us (2%)
    pallas_call x1, Pallas kernels, predict(): pl.pallas_call(lambda *refs: predict_kernel(facets, ncol, *refs), out_sha...  17.5 us
    pallas_call x1, Pallas kernels, form_image(): pl.pallas_call(image_kernel, out_shape=jax.ShapeDtypeStruct((2 * width, l...  13.7 us
    unnamed x17, local copies, waits for them, and re-layouts  3.75 us
    broadcast_in_dim x1, local copies, waits for them, and re-layouts, body(): offsets = sub_offset[:, :, None]  0.79 us

profile of v2, /device:TPU:0, one launch (start us, length us, event | category | flops | bytes accessed | tf_op | source)
XLA Modules:
  0.0 36.5 jit_solution(16953869431410040717)
XLA Ops:
  0.6 0.0 copy-start.5
  0.6 0.0 copy-start.6
  0.7 0.0 copy-start.7
  0.7 0.8 %copy.10.refs_3_.off_ref = s32[4,8,1]{2,1,0:T(8,128)S(1)} copy(s32[4,8,1]{1,0,2:T(4,128)} %bitcast.11) | data formatting | bytes 256 | tf_op jit(solution)/shard_map/broadcast_in_dim | solution.py:305
  1.5 0.0 copy-done.5
  1.5 0.0 copy-done.6
  1.5 0.0 copy-done.7
  1.5 0.0 copy-start
  1.5 1.1 %copy-done = f32[8,96,256]{2,1,0:T(8,128)S(1)} copy-done((f32[8,96,256]{2,1,0:T(8,128)S(1)}, f32[8,96,256]{2,1,0:T(8,128)}, u32[]{:S(2)}) %copy-start) | copy-done | bytes 786456
  2.6 0.0 copy-start.2
  2.6 1.1 %copy-done.2 = f32[1,2,48,2048]{3,2,1,0:T(8,128)S(1)} copy-done((f32[1,2,48,2048]{3,2,1,0:T(8,128)S(1)}, f32[1,2,48,2048]{3,2,1,0:T(8,128)}, u32[]{:S(2)}) %copy-start.2) | copy-done | bytes 786456
  3.7 0.0 copy-start.4
  3.7 0.9 %copy-done.4 = f32[128,256]{1,0:T(8,128)S(1)} copy-done((f32[128,256]{1,0:T(8,128)S(1)}, f32[128,256]{1,0:T(8,128)}, u32[]{:S(2)}) %copy-start.4) | copy-done | bytes 131096
  4.6 0.0 copy-start.1
  4.6 0.0 copy-start.3
  4.6 17.5 %shard_map.95 = (f32[4,8,2,128]{3,2,1,0:T(2,128)S(1)}, s32[4,8,2,128]{3,2,1,0:T(2,128)S(1)}, f32[2,128]{1,0:T(2,128)S(1)}) custom-call(f32[2,48,2048]{2,1,0:T(8,128)S(1)} %bitcast.6, s32[2,128]{1,0:T(2,128)S(1)} %bitcast.8, f32[2,128]{1,0:T(2,128)S(1)} %bitcast.9, s32[4,8,1]{2,1,0:T(8,128)S(1)} %copy.10.refs_3_.off_ref, f32[8,96,256]{2,1,0:T(8,128)S(1)} %copy-done, ...), custom_call_target="tpu_custom_call" | custom-call | tf_op jit(solution)/shard_map/pallas_call | solution.py:177
  22.2 0.0 copy-done.1
  22.2 0.0 copy-done.3
  22.2 13.7 %shard_map.96 = f32[96,2048]{1,0:T(8,128)} custom-call(f32[4,8,2,128]{3,2,1,0:T(2,128)S(1)} %get-tuple-element.5.res_ref, s32[4,8,2,128]{3,2,1,0:T(2,128)S(1)} %get-tuple-element.6.uv_ref, s32[4,8,1]{2,1,0:T(8,128)S(1)} %copy.10.refs_3_.off_ref, f32[8,96,256]{2,1,0:T(8,128)S(1)} %copy-done.1, f32[4,4,96,96]{3,2,1,0:T(8,128)S(1)} %copy-done.3, ...), custom_call_target="tpu_custom_call" | custom-call | tf_op jit(solution)/shard_map/pallas_call | solution.py:267
  35.9 0.6 %copy.13 = f32[1,1,2,128]{3,2,1,0:T(2,128)} copy(f32[1,1,2,128]{3,2,1,0:T(2,128)S(1)} %bitcast.7) | data formatting | bytes 2048
Async XLA Ops:
  0.6 0.8 %copy-start.5 = (f32[16,256]{1,0:T(8,128)S(1)}, f32[16,256]{1,0:T(8,128)}, u32[]{:S(2)}) copy-start(f32[16,256]{1,0:T(8,128)} %constant.9.clone.refs_6_.turn_ref) | copy-start | bytes 49156
  0.6 0.8 %copy-start.6 = (s32[1,1,2,128]{3,2,1,0:T(2,128)S(1)}, s32[1,1,2,128]{3,2,1,0:T(2,128)}, u32[]{:S(2)}) copy-start(s32[1,1,2,128]{3,2,1,0:T(2,128)} %param.10) | copy-start | bytes 3076
  0.7 0.8 %copy-start.7 = (f32[1,1,2,128]{3,2,1,0:T(2,128)S(1)}, f32[1,1,2,128]{3,2,1,0:T(2,128)}, u32[]{:S(2)}) copy-start(f32[1,1,2,128]{3,2,1,0:T(2,128)} %param.11) | copy-start | bytes 3076
  1.5 1.1 %copy-start = (f32[8,96,256]{2,1,0:T(8,128)S(1)}, f32[8,96,256]{2,1,0:T(8,128)}, u32[]{:S(2)}) copy-start(f32[8,96,256]{2,1,0:T(8,128)} %constant.10.clone.refs_4_.h_ref) | copy-start | bytes 2359300
  2.6 1.1 %copy-start.2 = (f32[1,2,48,2048]{3,2,1,0:T(8,128)S(1)}, f32[1,2,48,2048]{3,2,1,0:T(8,128)}, u32[]{:S(2)}) copy-start(f32[1,2,48,2048]{3,2,1,0:T(8,128)} %param.8) | copy-start | bytes 2359300
  3.7 0.9 %copy-start.4 = (f32[128,256]{1,0:T(8,128)S(1)}, f32[128,256]{1,0:T(8,128)}, u32[]{:S(2)}) copy-start(f32[128,256]{1,0:T(8,128)} %constant.8.clone.refs_5_.wave_ref) | copy-start | bytes 393220
  4.6 17.5 %copy-start.1 = (f32[8,96,256]{2,1,0:T(8,128)S(1)}, f32[8,96,256]{2,1,0:T(8,128)}, u32[]{:S(2)}) copy-start(f32[8,96,256]{2,1,0:T(8,128)} %constant.10.clone.refs_4_.h_ref) | copy-start | bytes 2359300
  4.6 17.5 %copy-start.3 = (f32[4,4,96,96]{3,2,1,0:T(8,128)S(1)}, f32[4,4,96,96]{3,2,1,0:T(8,128)}, u32[]{:S(2)}) copy-start(f32[4,4,96,96]{3,2,1,0:T(8,128)} %constant.11.clone.pm_ref) | copy-start | bytes 1769476

commit v3 on v2

--- a/solution.py
+++ b/solution.py
@@ -58,14 +58,14 @@
     cells = lax.broadcasted_iota(jnp.int32, (SUBGRID_SIZE, index.shape[1]), 0)
     hot = jnp.where(cells == index, 1.0, 0.0).astype(jnp.bfloat16)
     dims = (((1,), (0,)), ((), ()))
-    high, low = [lax.dot_general(p, hot, dims, preferred_element_type=jnp.float32) for p in parts]
-    return high + low
+    both = lax.dot_general(parts, hot, dims, preferred_element_type=jnp.float32)
+    return both[: both.shape[0] // 2] + both[both.shape[0] // 2 :]
 
 
 def predict_kernel(
-    facets, ncol, x_ref, uv_ref, meas_ref, off_ref, h_ref, wave_ref, turn_ref,
-    res_ref, all_uv_ref, own_ref,
-    uv_slots, uv_held, part_ref, slots, held, grid_ref, kt_ref, s1, r1, s2, r2, s3, r3, s4, r4,
+    facets, ncol, x_ref, uv_ref, meas_ref, off_ref, h_ref, pm_ref, wave_ref, turn_ref,
+    o_ref, own_ref,
+    uv_slots, uv_held, part_ref, slots, held, grid_ref, kt_ref, hot_ref, pg_ref, gv_ref, s1, r1, s2, r2, s3, r3, s4, r4,
 ):
     f = lax.axis_index("facet")
     c = lax.axis_index("col")
@@ -121,7 +121,8 @@
         p = dot3(z, wave_ref[...], ((1,), (0,)))
         grid_ref[:width, spans[rho]] = p[:width, :lanes] - p[width:, lanes:]
         grid_ref[width:, spans[rho]] = -(p[:width, lanes:] + p[width:, :lanes])
-    hot = placed(off_ref[c], width, length, lanes)
+    hot_ref[c] = placed(off_ref[c], width, length, lanes)
+    hot = hot_ref[c]
     dims = (((1,), (1,)), ((), ()))
     high, low = [
         lax.dot_general(hot, part, dims, preferred_element_type=jnp.float32)
@@ -135,7 +136,7 @@
         uv_held[c, lax.rem(f - d + facets, facets)] = uv_slots[d - 1]
     uv_later = over_columns(uv_held, s2, r2)
 
-    parts = split(h_ref[f])
+    parts = jnp.concatenate(split(h_ref[f]), axis=0)
     for s in range(facets):
         gu = picked(parts, uv_held[c, s, 0:1, :])
         gv = picked(parts, uv_held[c, s, 1:2, :])
@@ -152,6 +153,13 @@
         part_ref[s] = jnp.where(f == s, meas_ref[...], 0.0) - pred
 
     copies = over_facets(part_ref, slots, s3, r3)
+
+    def place_column(i, carry):
+        col = lax.rem(c + i, ncol)
+        hot_ref[col] = placed(off_ref[col], width, length, lanes)
+        return carry
+
+    lax.fori_loop(1, ncol, place_column, 0)
     total = part_ref[...]
     for d in range(1, facets):
         copies[d - 1].wait_recv()
@@ -159,17 +167,26 @@
     held[c] = total
     later = over_columns(held, s4, r4)
     own_ref[...] = held[c, f]
+    for copy in uv_later:
+        copy.wait()
+
+    def pick_column(col, carry):
+        phase = jnp.concatenate(split(dot3(pm_ref[c, col], h_ref[f], ((1,), (0,)))), axis=0)
+        for s in range(facets):
+            pg_ref[col, s] = picked(phase, uv_held[col, s, 0:1, :])
+            gv_ref[col, s] = picked(parts, uv_held[col, s, 1:2, :])
+        return carry
+
+    lax.fori_loop(0, ncol, pick_column, 0)
     for copy in uv_copies + copies:
         copy.wait_send()
-    for copy in uv_later:
-        copy.wait()
-    all_uv_ref[...] = uv_held[...]
     for copy in later:
         copy.wait()
-    res_ref[...] = held[...]
-
-
-def predict(x, uv, measured, offsets, h, wave, turn, facets, ncol):
+    grid_ref[...] = jnp.zeros_like(grid_ref)
+    form_image(held, pg_ref, gv_ref, hot_ref, wave_ref, turn_ref, o_ref, kt_ref, grid_ref)
+
+
+def predict(x, uv, measured, offsets, h, pm, wave, turn, facets, ncol):
     width, length = x.shape[1:]
     pair = uv.shape
     full = (ncol, facets) + pair
@@ -177,12 +194,11 @@
     return pl.pallas_call(
         lambda *refs: predict_kernel(facets, ncol, *refs),
         out_shape=(
-            jax.ShapeDtypeStruct(full, jnp.float32),
-            jax.ShapeDtypeStruct(full, jnp.int32),
+            jax.ShapeDtypeStruct((2 * width, length), jnp.float32),
             jax.ShapeDtypeStruct(pair, jnp.float32),
         ),
-        in_specs=[pl.BlockSpec(memory_space=pltpu.VMEM)] * 7,
-        out_specs=[pl.BlockSpec(memory_space=pltpu.VMEM)] * 3,
+        in_specs=[pl.BlockSpec(memory_space=pltpu.VMEM)] * 8,
+        out_specs=[pl.BlockSpec(memory_space=pltpu.VMEM)] * 2,
         scratch_shapes=[
             pltpu.VMEM((facets - 1,) + pair, jnp.int32),
             pltpu.VMEM(full, jnp.int32),
@@ -191,15 +207,18 @@
             pltpu.VMEM(full, jnp.float32),
             pltpu.VMEM((2 * width, length), jnp.float32),
             pltpu.VMEM((facets * width, 2 * width), jnp.float32),
+            pltpu.VMEM((ncol, facets * width, length), jnp.bfloat16),
+            pltpu.VMEM((ncol, facets, 2 * width, pair[1]), jnp.float32),
+            pltpu.VMEM((ncol, facets, 2 * width, pair[1]), jnp.float32),
         ]
         + [dma((facets - 1,))] * 2
         + [dma((ncol - 1,))] * 2
         + [dma((facets - 1,))] * 2
         + [dma((ncol - 1,))] * 2,
         compiler_params=pltpu.CompilerParams(
-            collective_id=1, has_side_effects=True, vmem_limit_bytes=48 * 2**20
+            collective_id=1, has_side_effects=True, vmem_limit_bytes=56 * 2**20
         ),
-    )(x, uv, measured, offsets, h, wave, turn)
+    )(x, uv, measured, offsets, h, pm, wave, turn)
 
 
 def small_dft(terms):
@@ -220,21 +239,15 @@
     return first + second
 
 
-def image_kernel(res_ref, uv_ref, off_ref, h_ref, pm_ref, wave_ref, turn_ref, o_ref, d_ref, grid_ref):
+def form_image(res_ref, pg_ref, gv_ref, hot_ref, wave_ref, turn_ref, o_ref, d_ref, grid_ref):
     ncol, per_col = res_ref.shape[:2]
-    width = h_ref.shape[1] // 2
-    h = h_ref[lax.axis_index("facet")]
-    rows = lax.axis_index("col")
-    parts = split(h)
+    width = o_ref.shape[0] // 2
     length = o_ref.shape[1]
     lanes = wave_ref.shape[0]
-    grid_ref[...] = jnp.zeros_like(grid_ref)
 
     def column(c, carry):
-        phase = split(dot3(pm_ref[rows, c], h, ((1,), (0,))))
         for s in range(per_col):
-            pg = picked(phase, uv_ref[c, s, 0:1, :])
-            gv = picked(parts, uv_ref[c, s, 1:2, :])
+            pg, gv = pg_ref[c, s], gv_ref[c, s]
             rr, ri = res_ref[c, s, 0:1, :], res_ref[c, s, 1:2, :]
             pr, pi = pg[:width], pg[width:]
             qr, qi = pr * rr - pi * ri, pr * ri + pi * rr
@@ -243,7 +256,7 @@
             )
             g = jnp.concatenate([gv[:width], gv[width:]], axis=1)
             d_ref[s * width : (s + 1) * width, :] = dot3(g, q, ((1,), (1,)))
-        hot = placed(off_ref[c], width, length, lanes)
+        hot = hot_ref[c]
         dims = (((1,), (0,)), ((), ()))
         for part in split(d_ref[...].T):
             grid_ref[...] += lax.dot_general(part, hot, dims, preferred_element_type=jnp.float32)
@@ -260,21 +273,6 @@
     for j, (r, i) in enumerate(small_dft(terms)):
         o_ref[:width, j * lanes : (j + 1) * lanes] = r
         o_ref[width:, j * lanes : (j + 1) * lanes] = i
-
-
-def form_image(res, uv, offsets, h, pm, wave, turn, width, length):
-    per_col = offsets.shape[1]
-    return pl.pallas_call(
-        image_kernel,
-        out_shape=jax.ShapeDtypeStruct((2 * width, length), jnp.float32),
-        in_specs=[pl.BlockSpec(memory_space=pltpu.VMEM)] * 7,
-        out_specs=pl.BlockSpec(memory_space=pltpu.VMEM),
-        scratch_shapes=[
-            pltpu.VMEM((per_col * width, 2 * width), jnp.float32),
-            pltpu.VMEM((2 * width, length), jnp.float32),
-        ],
-        compiler_params=pltpu.CompilerParams(vmem_limit_bytes=48 * 2**20),
-    )(res, uv, offsets, h, pm, wave, turn)
 
 
 def sides(z, axis):
@@ -303,10 +301,9 @@
         axis=2,
     ).astype(np.float32)
     offsets = sub_offset[:, :, None]
-    res, uv, own = predict(
-        strips[0], uv_cells[0, 0], measured[0, 0], offsets, h, wave, turn, facets, ncol
+    image, own = predict(
+        strips[0], uv_cells[0, 0], measured[0, 0], offsets, h, jnp.asarray(pm), wave, turn, facets, ncol
     )
-    image = form_image(res, uv, offsets, h, jnp.asarray(pm), wave, turn, width, length)
     return image.reshape(1, 2, width, length), own[None, None]
 
 

time: 36.7 us -> 30.9 us (0.84)
  Pallas kernels: 31.2 us -> 26 us
  local copies, waits for them, and re-layouts: 4.54 us -> 4.01 us
    pallas_call x1 -> x0, Pallas kernels: 13.7 us -> none  [form_image(): pl.pallas_call(image_kernel, out_shape=jax.ShapeDtypeStruct((2 * width, l...]
    pallas_call x1, Pallas kernels: 17.5 us -> 26 us  [predict(): pl.pallas_call(lambda *refs: predict_kernel(facets, ncol, *refs), out_sha...]
    unnamed x17 -> x6, local copies, waits for them, and re-layouts: 3.75 us -> 3.3 us
where the time goes in v3:
time: 30.9 us; the launch traced here: 30.7 us
  Pallas kernels  26 us (84%)
  local copies, waits for them, and re-layouts  4.01 us (13%)
  between operations  0.66 us (2%)
    pallas_call x1, Pallas kernels, predict(): pl.pallas_call(lambda *refs: predict_kernel(facets, ncol, *refs), out_sha...  26 us
    unnamed x6, local copies, waits for them, and re-layouts  3.3 us
    broadcast_in_dim x1, local copies, waits for them, and re-layouts, body(): offsets = sub_offset[:, :, None]  0.7 us

profile of v3, /device:TPU:0, one launch (start us, length us, event | category | flops | bytes accessed | tf_op | source)
XLA Modules:
  0.0 30.7 jit_solution(7791260239324270271)
XLA Ops:
  0.6 0.0 copy-start
  0.6 0.7 %copy-done = s32[4,8]{1,0:T(4,128)S(1)} copy-done((s32[4,8]{1,0:T(4,128)S(1)}, s32[4,8]{1,0:T(4,128)}, u32[]{:S(2)}) %copy-start) | copy-done | bytes 152
  1.3 0.7 %copy.10.refs_3_ = s32[4,8,1]{2,1,0:T(8,128)} copy(s32[4,8,1]{1,0,2:T(4,128)S(1)} %bitcast.8) | data formatting | bytes 256 | tf_op jit(solution)/shard_map/broadcast_in_dim | solution.py:303
  2.0 26.0 %shard_map.95 = (f32[96,2048]{1,0:T(8,128)}, f32[2,128]{1,0:T(2,128)}) custom-call(f32[2,48,2048]{2,1,0:T(8,128)} %bitcast.7, s32[2,128]{1,0:T(2,128)} %bitcast.9, f32[2,128]{1,0:T(2,128)} %bitcast.10, s32[4,8,1]{2,1,0:T(8,128)} %copy.10.refs_3_, f32[8,96,256]{2,1,0:T(8,128)} %constant.10.clone.refs_4_, f32[4,4,96,96]{3,2,1,0:T(8,128)} %constant.11.clone.refs_5_, ...), custom_call_target="tpu_custom_call" | custom-call | tf_op jit(solution)/shard_map/pallas_call | solution.py:194
  28.0 0.0 copy-start.1
  28.0 2.1 %copy.13 = f32[1,2,48,2048]{3,2,1,0:T(8,128)} copy(f32[1,2,48,2048]{3,2,1,0:T(8,128)} %bitcast.6) | data formatting | bytes 1572864
  30.1 0.0 copy-done.1
  30.1 0.6 %copy.14 = f32[1,1,2,128]{3,2,1,0:T(2,128)} copy(f32[1,1,2,128]{3,2,1,0:T(2,128)S(1)} %bitcast.11) | data formatting | bytes 2048
Async XLA Ops:
  0.6 0.7 %copy-start = (s32[4,8]{1,0:T(4,128)S(1)}, s32[4,8]{1,0:T(4,128)}, u32[]{:S(2)}) copy-start(s32[4,8]{1,0:T(4,128)} %param.9) | copy-start | bytes 388
  28.0 2.1 %copy-start.1 = (f32[2,128]{1,0:T(2,128)S(1)}, f32[2,128]{1,0:T(2,128)}, u32[]{:S(2)}) copy-start(f32[2,128]{1,0:T(2,128)} %get-tuple-element.5) | copy-start | bytes 3076
